TPU v7x, 32 devices: a whole 2x2x4 slice. The times are simulated.
32 devices in a mesh: row: 8 (over z, core), col: 4 (over y, x).
Axes of the slice: x: 2, y: 2, z: 4, core: 2. Of those that a mesh axis runs over, the one named last changes fastest.
Arguments:
- tile_values: float32 [1536, 32, 1024], P(('row', 'col')), may hold values from -6 to 6
- tile_count: int32 [32], P(('row', 'col')), may hold values from 1 to 48, as said below
- mode1_column: int32 [1536, 1], P(('row', 'col')), may hold values from 0 to 3; in each aligned block of 48 rows (0 to 47, 48 to 95, ...) at most 13 rows name the same one
- mode1_offset: int32 [1536], P(('row', 'col')), may hold values from 0 to 15
- mode2_row: int32 [1536, 1], P(('row', 'col')), may hold values from 0 to 7; in each aligned block of 48 rows (0 to 47, 48 to 95, ...) at most 7 rows name the same one
- mode2_offset: int32 [1536], P(('row', 'col')), may hold values from 0 to 7
- mode3_offset: int32 [1536], P(('row', 'col')), may hold values from 0 to 15
- mode2_factor: float32 [8192, 256], P(('row', 'col'))
- mode3_factor: float32 [2048, 256], P('col')
Outputs:
- updated: float32 [16384, 256], P(('row', 'col'))
Inputs may be any that keep to these rules, and one draw needn't show every extreme that they name: Device d's live tiles fill its first tile_count[d] slots; other slots are ignored. Some device holds 48 live tiles. `mode1_column`: at most 13 slots of one device name the same value, and some device reaches it. `mode2_row`: at most 7 slots of one device name the same value, and some device reaches it.
All inputs are finite; a program needn't handle non-finite values.
Results may differ from a plain program's by a relative error of at most 0.0003.
Values sent between devices are 32-bit elements; how exact they have to be, the bound alone decides.
A program may use at most 128 MiB of HBM per device.

v0:
```python
import jax
import jax.numpy as jnp
from jax import lax
from jax.sharding import PartitionSpec as P

IB_DEV = 16


HIGHEST_PRECISION = lax.Precision.HIGHEST


def product_of(left_matrix, right_matrix):
    return lax.dot_general(
        left_matrix,
        right_matrix,
        (((0,), (0,)), ((), ())),
        precision=HIGHEST_PRECISION,
        preferred_element_type=jnp.float32,
    )


def local(
    tile_values,
    tile_count,
    mode1_column,
    mode1_offset,
    mode2_row,
    mode2_offset,
    mode3_offset,
    mode2_factor,
    mode3_factor,
):
    slot_count = tile_values.shape[0]
    tile_edge = tile_values.shape[1]
    rank_width = mode2_factor.shape[1]
    rows_held = mode2_factor.shape[0]
    col_index = lax.axis_index("col")
    live_count = tile_count[0]
    slot_index = jnp.arange(slot_count, dtype=jnp.int32)
    is_live = slot_index < live_count
    tile_lines = jnp.arange(tile_edge, dtype=jnp.int32)
    owner_row = jnp.where(is_live, mode2_row[:, 0], -1)
    owner_col = jnp.where(is_live, mode1_column[:, 0], -1)
    own_second = product_of(mode2_factor, mode2_factor)
    own_third = product_of(mode3_factor, mode3_factor)
    sum_second = lax.psum(own_second, ("row", "col"))
    sum_third = lax.psum(own_third, "col")
    normal_matrix = sum_second * sum_third
    wanted = (owner_row * rows_held + mode2_offset * tile_edge)[:, None] + tile_lines[None, :]
    shard_piece = lax.all_gather(mode2_factor, "row", axis=0, tiled=True)
    piece_length = shard_piece.shape[0]
    inside = (wanted >= 0) & (wanted < piece_length)
    taken = jnp.take(shard_piece, jnp.clip(wanted, 0, piece_length - 1).reshape(-1), axis=0)
    taken = taken.reshape(slot_count, tile_edge, rank_width)
    picked = jnp.where(inside[:, :, None], taken, 0.0)
    third_index = (mode3_offset * tile_edge)[:, None] + tile_lines[None, :]
    mode3_rows = jnp.take(mode3_factor, third_index.reshape(-1), axis=0).reshape(
        slot_count, tile_edge, rank_width
    )
    group_size = min(8, slot_count)
    group_total = (live_count + group_size - 1) // group_size

    def contract(group_at, partials):
        start_slot = jnp.minimum(group_at * group_size, slot_count - group_size).astype(jnp.int32)
        second_part = lax.dynamic_slice_in_dim(picked, start_slot, group_size, 0)
        third_part = lax.dynamic_slice_in_dim(mode3_rows, start_slot, group_size, 0)
        values_part = lax.dynamic_slice_in_dim(tile_values, start_slot, group_size, 0)
        khatri = (second_part[:, :, None, :] * third_part[:, None, :, :]).reshape(
            group_size, tile_edge * tile_edge, rank_width
        )
        product_rows = jnp.einsum("gie,ger->gir", values_part, khatri, precision=HIGHEST_PRECISION)
        return lax.dynamic_update_slice_in_dim(partials, product_rows, start_slot, 0)

    partials = lax.fori_loop(
        0, group_total, contract, jnp.zeros((slot_count, tile_edge, rank_width), jnp.float32)
    )
    sent_targets = jnp.where(is_live, owner_col * IB_DEV + mode1_offset, -1).astype(jnp.float32)
    own_blocks = (col_index * IB_DEV + jnp.arange(IB_DEV, dtype=jnp.int32)).astype(jnp.float32)
    gathered_rows = lax.all_gather(partials, "col", axis=0, tiled=True)
    gathered_targets = lax.all_gather(sent_targets, "col", axis=0, tiled=True)
    selector = (gathered_targets[:, None] == own_blocks[None, :]).astype(jnp.float32)
    mttkrp = jnp.einsum("pb,pir->bir", selector, gathered_rows, precision=HIGHEST_PRECISION)
    cholesky_factor = jnp.linalg.cholesky(normal_matrix)
    mttkrp_rows = mttkrp.reshape(IB_DEV * tile_edge, rank_width)
    return jax.scipy.linalg.cho_solve((cholesky_factor, True), mttkrp_rows.T).T


def solution(mesh):
    placed = (
        P(("row", "col"), None, None),
        P(("row", "col")),
        P(("row", "col"), None),
        P(("row", "col")),
        P(("row", "col"), None),
        P(("row", "col")),
        P(("row", "col")),
        P(("row", "col"), None),
        P("col", None),
    )
    return jax.shard_map(
        local, mesh=mesh, in_specs=placed, out_specs=P(("row", "col"), None), check_vma=False
    )
```

profile of v0, /device:TPU:0, one launch (start us, length us, event | category | flops | bytes accessed | tf_op | source)
XLA Modules:
  0.0 284.2 jit_solution(9556481128477041025)
XLA Ops:
  7.4 0.7 all-gather.3.cloned.1.call-update
  8.2 2.3 fusion.31
  10.6 1.7 fusion.32
  13.7 3.7 %gather_fusion.1 = f32[1536,256]{1,0:T(8,128)S(1)} fusion(f32[512,256]{1,0:T(8,128)S(1)} %copy-done, s32[2048]{0:T(1024)S(1)} %pad_clamp_fusion), kind=kCustom, calls=%fused_computation.1 | custom fusion | bytes 3151872 | tf_op jit(solution)/shard_map/jit(_take)/gather | solution.py:57
  17.4 1.4 broadcast_select_fusion
  18.8 23.7 %all-gather.3.cloned.1.call-done = f32[2048,256]{1,0:T(8,128)} async-done(((f32[256,256]{1,0:T(8,128)}), f32[2048,256]{1,0:T(8,128)}) %all-gather.3.cloned.1.call-update) | async-done | bytes 2097168 | tf_op jit(solution)/shard_map/all_gather | solution.py:50
  42.5 5.3 %gather_fusion = f32[1536,256]{1,0:T(8,128)S(1)} fusion(f32[2048,256]{1,0:T(8,128)} %all-gather.3.cloned.1.call-done, s32[2048]{0:T(1024)S(1)} %pad_clamp_fusion.1), kind=kCustom, calls=%fused_computation | custom fusion | bytes 3151872 | tf_op jit(solution)/shard_map/jit(_take)/gather | solution.py:53
  47.8 1.5 select_select_fusion
  49.2 0.2 broadcast_in_dim.49.clone
  49.4 44.2 %while.11 = (s32[]{:T(128)}, f32[48,32,256]{2,0,1:T(8,128)S(1)}, s32[]{:T(128)}, f32[48,32,1024]{2,1,0:T(8,128)}, f32[48,32,256]{2,1,0:T(8,128)}, /*index=5*/f32...) while((s32[]{:T(128)}, f32[48,32,256]{2,0,1:T(8,128)S(1)}, ...), condition=%wide.region_7.8_spmd, body=%wide.region_6.7_spmd.sunk | while | flops 807403520 | bytes 20709556 | solution.py:74
  49.4 1.1 constant_dynamic-slice_fusion.5
  50.5 1.2 broadcast_multiply_fusion.3
  51.7 6.1 %fusion.52 = f32[8,32,256]{2,1,0:T(8,128)S(1)} fusion(f32[8,1024,256]{2,1,0:T(8,128)S(1)} %bitcast.78, f32[48,32,1024]{2,1,0:T(8,128)} %get-tuple-element.177, s32[]{:T(128)S(6)} %select_n.118), kind=kOutput, calls=%fused_computation.3.clone.1 | convolution fusion | flops 805306368 | bytes 9699332 | tf_op jit(solution)/shard_map/while/body/gie,ger->gir/dot_general | solution.py:71
  57.8 0.2 copy.29
  58.0 0.3 dynamic_update_slice.4
  58.3 1.1 constant_dynamic-slice_fusion.5
  59.4 1.2 broadcast_multiply_fusion.3
  60.5 6.1 %fusion.52 = f32[8,32,256]{2,1,0:T(8,128)S(1)} fusion(f32[8,1024,256]{2,1,0:T(8,128)S(1)} %bitcast.78, f32[48,32,1024]{2,1,0:T(8,128)} %get-tuple-element.177, s32[]{:T(128)S(6)} %select_n.118), kind=kOutput, calls=%fused_computation.3.clone.1 | convolution fusion | flops 805306368 | bytes 9699332 | tf_op jit(solution)/shard_map/while/body/gie,ger->gir/dot_general | solution.py:71
  66.6 0.2 copy.29
  66.8 0.3 dynamic_update_slice.4
  67.1 1.1 constant_dynamic-slice_fusion.5
  68.2 1.2 broadcast_multiply_fusion.3
  69.4 6.1 %fusion.52 = f32[8,32,256]{2,1,0:T(8,128)S(1)} fusion(f32[8,1024,256]{2,1,0:T(8,128)S(1)} %bitcast.78, f32[48,32,1024]{2,1,0:T(8,128)} %get-tuple-element.177, s32[]{:T(128)S(6)} %select_n.118), kind=kOutput, calls=%fused_computation.3.clone.1 | convolution fusion | flops 805306368 | bytes 9699332 | tf_op jit(solution)/shard_map/while/body/gie,ger->gir/dot_general | solution.py:71
  75.5 0.2 copy.29
  75.6 0.3 dynamic_update_slice.4
  76.0 1.1 constant_dynamic-slice_fusion.5
  77.0 1.2 broadcast_multiply_fusion.3
  78.2 6.1 %fusion.52 = f32[8,32,256]{2,1,0:T(8,128)S(1)} fusion(f32[8,1024,256]{2,1,0:T(8,128)S(1)} %bitcast.78, f32[48,32,1024]{2,1,0:T(8,128)} %get-tuple-element.177, s32[]{:T(128)S(6)} %select_n.118), kind=kOutput, calls=%fused_computation.3.clone.1 | convolution fusion | flops 805306368 | bytes 9699332 | tf_op jit(solution)/shard_map/while/body/gie,ger->gir/dot_general | solution.py:71
  84.3 0.2 copy.29
  84.5 0.3 dynamic_update_slice.4
  84.8 1.1 constant_dynamic-slice_fusion.5
  85.9 1.2 broadcast_multiply_fusion.3
  87.0 6.1 %fusion.52 = f32[8,32,256]{2,1,0:T(8,128)S(1)} fusion(f32[8,1024,256]{2,1,0:T(8,128)S(1)} %bitcast.78, f32[48,32,1024]{2,1,0:T(8,128)} %get-tuple-element.177, s32[]{:T(128)S(6)} %select_n.118), kind=kOutput, calls=%fused_computation.3.clone.1 | convolution fusion | flops 805306368 | bytes 9699332 | tf_op jit(solution)/shard_map/while/body/gie,ger->gir/dot_general | solution.py:71
  93.2 0.2 copy.29
  93.3 0.3 dynamic_update_slice.4
  93.7 1.1 copy-done.1
  94.8 0.6 dynamic-slice.3
  96.3 10.0 %all-reduce.1 = f32[192]{0:T(256)S(1)} all-reduce(f32[192]{0:T(256)S(1)} %convert_dynamic-update-slice_fusion), channel_id=1, replica_groups=mesh['row'=8,'col'=4] {'col'}, use_global_device_ids=true, to_apply=%add.1 | all-reduce | flops 192 | bytes 1536
  106.2 45.2 %all-reduce.5.cloned.1.call-done = f32[256,256]{0,1:T(8,128)} async-done(((f32[256,256]{0,1:T(8,128)}), f32[256,256]{0,1:T(8,128)}) %all-reduce.5.cloned.1.call-update) | async-done | bytes 262160 | tf_op jit(solution)/shard_map/psum | solution.py:46
  151.4 44.3 %all-reduce.7.cloned.1.call-done = f32[256,256]{0,1:T(8,128)} async-done(((f32[256,256]{0,1:T(8,128)}), f32[256,256]{0,1:T(8,128)}) %all-reduce.7.cloned.1.call-update) | async-done | bytes 262160 | tf_op jit(solution)/shard_map/psum | solution.py:47
  195.7 1.1 mul.44
  196.8 0.1 copy.17
  197.0 11.7 %cholesky.50 = f32[128,128]{1,0:T(8,128)S(1)} custom-call(f32[128,128]{1,0:T(8,128)S(1)} %cholesky.118), custom_call_target="Cholesky" | custom-call | tf_op jit(solution)/shard_map/jit(cholesky)/cholesky | solution.py:83
  208.8 9.8 %custom-call.18 = f32[1,128,128]{1,2,0:T(8,128)S(1)} custom-call(f32[1,128,128]{2,1,0:T(8,128)S(1)} %get-tuple-element.74), custom_call_target="InvertDiagBlocksLowerTriangular" | custom-call | tf_op jit(solution)/shard_map/jit(cholesky)/cholesky | solution.py:83
  218.6 0.2 constant_dynamic-update-slice_fusion.1
  218.8 0.3 convolution_subtract_fusion.2
  219.1 11.7 %cholesky.105 = f32[128,128]{1,0:T(8,128)S(1)} custom-call(f32[128,128]{1,0:T(8,128)S(1)} %convolution_subtract_fusion.2), custom_call_target="Cholesky" | custom-call | tf_op jit(solution)/shard_map/jit(cholesky)/cholesky | solution.py:83
  230.8 0.7 compare_reduce_fusion
  233.0 4.1 %while.12 = (s32[]{:T(128)}, f32[256,256]{1,0:T(8,128)S(1)}, s32[2,2]{1,0:T(2,128)S(1)}, f32[2,128,128]{2,1,0:T(8,128)S(1)}, s32[]{:T(128)}) while((s32[]{:T(128)}, f32[256,256]{1,0:T(8,128)S(1)}, s32[2,2]{1,0:T(2,128)S(1)}, f32[2,128,128]{2,1,0:T(8,128)S(1)}, s32[]{:T(128)}) %tuple.43), condition=%wide.while_cond, body=%wide.while_body.sunk | while | flops 2 | bytes 131181 | solution.py:85
  233.0 0.6 fusion.53
  233.6 1.4 bitcast_dynamic-update-slice_fusion.2
  235.0 0.6 fusion.53
  235.6 1.4 bitcast_dynamic-update-slice_fusion.2
  237.0 19.9 %custom-call.19 = f32[2,128,128]{1,2,0:T(8,128)S(1)} custom-call(f32[2,128,128]{2,1,0:T(8,128)S(1)} %get-tuple-element.46), custom_call_target="InvertDiagBlocksLowerTriangular" | custom-call | tf_op jit(solution)/shard_map/jit(_cho_solve)/triangular_solve | solution.py:85
  256.9 10.8 %all-gather.5.cloned.1.call-done = f32[192,32,256]{2,0,1:T(8,128)} async-done(((f32[48,32,256]{2,0,1:T(8,128)}), f32[192,32,256]{2,0,1:T(8,128)}) %all-gather.5.cloned.1.call-update) | async-done | bytes 6291472 | tf_op jit(solution)/shard_map/all_gather | solution.py:79
  267.7 5.0 %fusion.18 = f32[16,32,256]{2,0,1:T(8,128)S(1)} fusion(f32[192,32,256]{2,0,1:T(8,128)} %all-gather.5.cloned.1.call-done, f32[192]{0:T(256)S(1)} %all-reduce.1, f32[16]{0:T(128)S(1)} %add_convert_fusion), kind=kOutput, calls=%fused_computation.49 | convolution fusion | flops 301992960 | bytes 6816576 | tf_op jit(solution)/shard_map/pb,pir->bir/dot_general | solution.py:82
  272.7 0.3 copy.19
  273.0 0.4 fusion.3
  273.4 0.6 convolution_subtract_fusion.1
  274.0 0.4 fusion.11
  274.4 0.4 fusion.10
  274.8 0.4 convolution_subtract_fusion
  275.2 0.4 fusion.9
  275.6 1.0 copy.20
  (49 shorter events, 1.2 us)
Async XLA Ops:
  7.4 3.2 %copy-start = (f32[512,256]{1,0:T(8,128)S(1)}, f32[512,256]{1,0:T(8,128)}, u32[]{:S(2)}) copy-start(f32[512,256]{1,0:T(8,128)} %param.19) | copy-start | bytes 1572868
  7.4 5.7 %copy-start.4 = (s32[48,1]{0,1:T(1,128)S(1)}, s32[48,1]{0,1:T(1,128)}, u32[]{:S(2)}) copy-start(s32[48,1]{0,1:T(1,128)} %param.15) | copy-start | bytes 580
  7.4 5.7 %copy-start.5 = (s32[48]{0:T(128)S(1)}, s32[48]{0:T(128)}, u32[]{:S(2)}) copy-start(s32[48]{0:T(128)} %param.16) | copy-start | bytes 580
  7.4 5.9 %copy-start.6 = (s32[48]{0:T(128)S(1)}, s32[48]{0:T(128)}, u32[]{:S(2)}) copy-start(s32[48]{0:T(128)} %param.17) | copy-start | bytes 580
  7.4 35.1 %all-gather.3.cloned.1.call-start = ((), (), s32[]{:S(2)}) async-start(), calls=%async_computation.2 | async-start | bytes 2359296 | tf_op jit(solution)/shard_map/all_gather | solution.py:50
  8.1 143.3 %all-reduce.5.cloned.1.call-start = ((), (), s32[]{:S(2)}) async-start(), calls=%async_computation | async-start | bytes 524288 | tf_op jit(solution)/shard_map/psum | solution.py:46
  10.5 185.2 %all-reduce.7.cloned.1.call-start = ((), (), s32[]{:S(2)}) async-start(), calls=%async_computation.1 | async-start | bytes 524288 | tf_op jit(solution)/shard_map/psum | solution.py:47
  12.3 255.4 %all-gather.5.cloned.1.call-start = ((), (), s32[]{:S(2)}) async-start(), calls=%async_computation.3 | async-start | bytes 7864320 | tf_op jit(solution)/shard_map/all_gather | solution.py:79
  93.6 1.1 copy-start.1
  93.6 1.2 copy-start.7
  93.7 2.5 copy-start.2
  93.7 2.5 copy-start.3
Sparse Core Ops, SparseCore 0:
  9.9 32.5 all-gather.2
Sparse Core Ops, SparseCore 1:
  14.1 137.3 all-reduce.4
  154.2 41.4 all-reduce.6
  197.6 70.1 all-gather.4
where the time goes:
time: 285 us; the launch traced here: 284 us
  waiting for transfers between devices  125 us (44%)
  other arithmetic  64.2 us (23%)
  matrix products  42.6 us (15%)
  local copies, waits for them, and re-layouts  24.2 us (8%)
  between operations  18 us (6%)
  blocking collectives  9.98 us (4%)
    psum x1, waiting for transfers between devices, local(): sum_second = lax.psum(own_second, ('row', 'col'))  45.2 us
    psum x1, waiting for transfers between devices, local(): sum_third = lax.psum(own_third, 'col')  44.3 us
    another operation x6, other arithmetic, local(): cholesky_factor = jnp.linalg.cholesky(normal_matrix)  34 us
    dot_general x5, matrix products, contract(): jnp.einsum('gie,ger->gir', values_part, khatri, precision=HIGHEST_PRECISION)  30.5 us
    all_gather x1, waiting for transfers between devices, local(): shard_piece = lax.all_gather(mode2_factor, 'row', axis=0, tiled=True)  23.7 us
    another operation x3, other arithmetic, local(): return jax.scipy.linalg.cho_solve((cholesky_factor, True), mttkrp_rows.T).T  19.9 us
    all_gather x1, waiting for transfers between devices, local(): gathered_rows = lax.all_gather(partials, 'col', axis=0, tiled=True)  10.8 us
    unnamed x1, blocking collectives  9.98 us
  transfers between devices with their start and end apart: 4, of which 4 were waited for; matrix products, arithmetic and copies ran while one was open for 43% of the time, Pallas kernels for 0%

commit v1 on v0

v1 whole, which is shorter than its diff:
```python
import functools

import jax
import jax.numpy as jnp
from jax import lax
from jax.experimental import pallas as pl
from jax.experimental.pallas import tpu as pltpu
from jax.sharding import PartitionSpec as P

IB_DEV = 16
PIVOT = 32
MESH = pl.DeviceIdType.MESH
HIGHEST = lax.Precision.HIGHEST


def exact_dot(left, right, contract=((1,), (0,))):
    return lax.dot_general(
        left, right, (contract, ((), ())), precision=HIGHEST, preferred_element_type=jnp.float32
    )


def split(values):
    high = values.astype(jnp.bfloat16)
    return high, (values - high.astype(jnp.float32)).astype(jnp.bfloat16)


def invert_small(block):
    size = block.shape[0]
    line = lax.broadcasted_iota(jnp.int32, (size, size), 0)
    lane = lax.broadcasted_iota(jnp.int32, (size, size), 1)
    lane_row = lax.broadcasted_iota(jnp.int32, (1, size), 1)
    for k in range(size):
        scale = 1.0 / block[k : k + 1, k : k + 1]
        row = jnp.where(lane_row == k, scale, block[k : k + 1, :] * scale)
        column = block[:, k : k + 1]
        kept = jnp.where(lane == k, 0.0, block)
        block = jnp.where(line == k, row, kept - column * row)
    return block


def eliminate(matrix, at):
    size = matrix.shape[0]
    start = at * PIVOT
    rows = matrix[start : start + PIVOT, :]
    columns = matrix[:, start : start + PIVOT]
    lane = lax.broadcasted_iota(jnp.int32, (PIVOT, size), 1)
    line = lax.broadcasted_iota(jnp.int32, (PIVOT, size), 0)
    inside = (lane >= start) & (lane < start + PIVOT)
    pivot = invert_small(rows[:, start : start + PIVOT])
    unit = jnp.where(lane - start == line, 1.0, 0.0)
    new_rows = exact_dot(pivot, jnp.where(inside, unit, rows))
    lane_all = lax.broadcasted_iota(jnp.int32, (size, size), 1)
    inside_all = (lane_all >= start) & (lane_all < start + PIVOT)
    rest = jnp.where(inside_all, 0.0, matrix) - exact_dot(columns, new_rows)
    pieces = [rest[:start], new_rows, rest[start + PIVOT :]]
    return jnp.concatenate([piece for piece in pieces if piece.shape[0]], axis=0)


def kernel(
    n_row,
    n_col,
    index_ref,
    live_ref,
    target_ref,
    x_hbm,
    b_ref,
    c_ref,
    out_ref,
    x_ref,
    b_all,
    c_high,
    c_low,
    gram2,
    gram3,
    gram_in,
    normal_in,
    partials,
    send,
    arrive,
    x_sem,
    line_send,
    line_recv,
    pair_send,
    pair_recv,
    gram_send,
    gram_recv,
    normal_send,
    normal_recv,
    block_send,
    block_recv,
):
    row = lax.axis_index("row")
    col = lax.axis_index("col")
    chip, core = row // 2, row % 2
    chips = n_row // 2
    other = chip * 2 + 1 - core
    slots, edge = x_ref.shape[0], x_ref.shape[1]
    rank = b_ref.shape[1]
    piece = rank // n_row
    rows_out = IB_DEV * edge
    held_blocks = b_ref.shape[0] // edge

    load_x = pltpu.make_async_copy(x_hbm, x_ref, x_sem)
    load_x.start()

    barrier = pltpu.get_barrier_semaphore()
    for step in range(1, n_row):
        pl.semaphore_signal(
            barrier, inc=1, device_id=((row + step) % n_row, col), device_id_type=MESH
        )
    for step in range(1, n_col):
        pl.semaphore_signal(
            barrier, inc=1, device_id=(row, (col + step) % n_col), device_id_type=MESH
        )
    b_all[pl.ds(row * held_blocks, held_blocks)] = b_ref[...].reshape(held_blocks, edge, rank)
    pl.semaphore_wait(barrier, n_row + n_col - 2)

    def line_copy(way, step, slot_chip, to_chip):
        held = pl.ds((slot_chip * 2 + core) * held_blocks, held_blocks)
        return pltpu.make_async_remote_copy(
            src_ref=b_all.at[held],
            dst_ref=b_all.at[held],
            send_sem=line_send.at[way, step],
            recv_sem=line_recv.at[way, step],
            device_id=(to_chip * 2 + core, col),
            device_id_type=MESH,
        )

    def pair_copy(number, slot_row):
        held = pl.ds(slot_row * held_blocks, held_blocks)
        return pltpu.make_async_remote_copy(
            src_ref=b_all.at[held],
            dst_ref=b_all.at[held],
            send_sem=pair_send.at[number],
            recv_sem=pair_recv.at[number],
            device_id=(other, col),
            device_id_type=MESH,
        )

    def has(way, step):
        return chip >= 1 + step if way == 0 else chip + 1 + step < chips

    def sends(way, step):
        if way == 0:
            return (chip < chips - 1) & (chip >= step)
        return (chip > 0) & (chip + step < chips)

    def sent_chip(way, step):
        return chip - step if way == 0 else chip + step

    def next_chip(way):
        return chip + 1 if way == 0 else chip - 1

    for way in range(2):

        @pl.when(sends(way, 0))
        def _():
            line_copy(way, 0, sent_chip(way, 0), next_chip(way)).start()

    pair_copy(0, row).start()

    third = c_ref[...]
    high, low = split(third)
    c_high[...] = high.reshape(c_high.shape)
    c_low[...] = low.reshape(c_low.shape)
    gram3[...] = exact_dot(third, third, ((0,), (0,)))
    own = b_ref[...]
    gram2[...] = exact_dot(own, own, ((0,), (0,)))
    pair_copy(0, other).wait_recv()

    def add_gram(slot_row):
        block = b_all[pl.ds(slot_row * held_blocks, held_blocks)].reshape(b_ref.shape)
        gram2[...] += exact_dot(block, block, ((0,), (0,)))

    add_gram(other)
    for step in range(chips - 1):
        for way in range(2):

            @pl.when(has(way, step))
            def _():
                held = sent_chip(way, step + 1)
                line_copy(way, step, held, next_chip(way)).wait_recv()
                pair_copy(1 + 2 * step + way, held * 2 + core).start()

            if step + 1 < chips - 1:

                @pl.when(sends(way, step + 1))
                def _():
                    line_copy(way, step + 1, sent_chip(way, step + 1), next_chip(way)).start()

        for way in range(2):

            @pl.when(has(way, step))
            def _():
                held = sent_chip(way, step + 1)
                add_gram(held * 2 + core)
                pair_copy(1 + 2 * step + way, held * 2 + 1 - core).wait_recv()
                add_gram(held * 2 + 1 - core)

    def gram_copy(step, which):
        to_col = (col + step) % n_col
        source = gram2 if which == 0 else gram3
        return pltpu.make_async_remote_copy(
            src_ref=source.at[pl.ds(pl.multiple_of(row * piece, 8), piece)],
            dst_ref=gram_in.at[which, step],
            send_sem=gram_send.at[which, step],
            recv_sem=gram_recv.at[which, step],
            device_id=(row, to_col),
            device_id_type=MESH,
        )

    for step in range(1, n_col):
        gram_copy(step, 0).start()
        gram_copy(step, 1).start()

    load_x.wait()
    lane = lax.broadcasted_iota(jnp.int32, (edge, 128), 1)
    lane_row = lax.broadcasted_iota(jnp.int32, (1, 128), 1) // edge
    one_mask = [jnp.where(lane_row == m, 1.0, 0.0).astype(jnp.bfloat16) for m in range(4)]
    two_mask = [jnp.where(lane_row % 2 == m, 1.0, 0.0).astype(jnp.bfloat16) for m in range(2)]
    chunks = edge * edge // 128

    def tile(t, carried):
        third_at = index_ref[1, t]
        weights_high = c_high[third_at]
        weights_low = c_low[third_at]
        weights = jnp.concatenate([weights_high] * 6 + [weights_low] * 2, axis=0)
        pieces = []
        for q in range(chunks):
            x = x_ref[t, :, q * 128 : (q + 1) * 128]
            first = x.astype(jnp.bfloat16)
            x_high = first.astype(jnp.float32)
            x_low = x - x_high
            turned_high = pltpu.roll(x_high, 64, 1)
            turned_low = pltpu.roll(x_low, 64, 1)
            front = jnp.where(lane < 64, x_low, turned_high).astype(jnp.bfloat16)
            back = jnp.where(lane < 64, turned_low, x_high).astype(jnp.bfloat16)
            for m in range(4):
                rest = front if m < 2 else back
                pieces.append(
                    jnp.concatenate([first * one_mask[m], rest * two_mask[m % 2]], axis=1)
                )
        inner = jnp.dot(
            jnp.concatenate(pieces, axis=0), weights, preferred_element_type=jnp.float32
        )
        second = b_all[index_ref[0, t]]
        total = inner[:edge] * second[0:1]
        for j in range(1, edge):
            total = total + inner[j * edge : (j + 1) * edge] * second[j : j + 1]
        partials[:, pl.ds(t, 1), :] = total[:, None, :]
        return carried

    lax.fori_loop(0, slots, tile, 0)

    for step in range(1, n_col):
        gram_copy(step, 0).wait_recv()
        gram_copy(step, 1).wait_recv()
    own_piece = pl.ds(pl.multiple_of(row * piece, 8), piece)
    sum2, sum3 = gram2[own_piece, :], gram3[own_piece, :]
    for step in range(1, n_col):
        sum2 = sum2 + gram_in[0, step]
        sum3 = sum3 + gram_in[1, step]
    normal_in[row] = sum2 * sum3

    def normal_copy(step, slot):
        return pltpu.make_async_remote_copy(
            src_ref=normal_in.at[slot],
            dst_ref=normal_in.at[slot],
            send_sem=normal_send.at[step],
            recv_sem=normal_recv.at[step],
            device_id=((row + step) % n_row, col),
            device_id_type=MESH,
        )

    for step in range(1, n_row):
        normal_copy(step, row).start()

    targets = n_col * IB_DEV
    chosen = lax.broadcasted_iota(jnp.int32, (targets, slots), 0) == target_ref[...]
    chosen = jnp.where(chosen, 1.0, 0.0)
    chosen = jnp.concatenate([chosen, chosen], axis=1).astype(jnp.bfloat16)

    live = live_ref[...] > 0

    def choose(i, carried):
        high, low = split(jnp.where(live, partials[i], 0.0))
        rows = jnp.dot(
            chosen, jnp.concatenate([high, low], axis=0), preferred_element_type=jnp.float32
        )
        for c in range(n_col):
            send[c, pl.ds(pl.multiple_of(i * IB_DEV, IB_DEV), IB_DEV), :] = rows[
                c * IB_DEV : (c + 1) * IB_DEV
            ]
        return carried

    lax.fori_loop(0, edge, choose, 0)

    def block_copy(number, source, target, to_col):
        return pltpu.make_async_remote_copy(
            src_ref=source,
            dst_ref=target,
            send_sem=block_send.at[number],
            recv_sem=block_recv.at[number],
            device_id=(row, to_col),
            device_id_type=MESH,
        )

    half = rows_out // 2
    halves = (pl.ds(0, half), pl.ds(half, half))
    copies = []
    later = []
    if n_col == 4:
        near = (col // 2) * 2 + 1 - col % 2
        far = (1 - col // 2) * 2 + col % 2
        corner = (1 - col // 2) * 2 + 1 - col % 2
        sides = (near, far)
        for way in range(2):
            copies.append(
                block_copy(way, send.at[corner, halves[way]], arrive.at[0, halves[way]], sides[way])
            )
        for way in range(2):
            copies.append(
                block_copy(2 + way, send.at[sides[way], halves[way]], arrive.at[1, halves[way]], sides[way])
            )
        for way in range(2):
            later.append(
                block_copy(4 + way, send.at[sides[1 - way], halves[way]], arrive.at[2, halves[way]], sides[1 - way])
            )
    else:
        for step in range(1, n_col):
            to_col = (col + step) % n_col
            copies.append(block_copy(step - 1, send.at[to_col], arrive.at[step - 1], to_col))
    for copy in copies:
        copy.start()

    for step in range(1, n_row):
        normal_copy(step, (row + n_row - step) % n_row).wait_recv()
    matrix = jnp.concatenate([normal_in[r] for r in range(n_row)], axis=0)
    pivots = rank // PIVOT
    for at in range(pivots // 2):
        matrix = eliminate(matrix, at)
    if later:
        for way in range(2):
            copies[way].wait_recv()
            send[sides[1 - way], halves[way]] += arrive[0, halves[way]]
            later[way].start()
    for at in range(pivots // 2, pivots):
        matrix = eliminate(matrix, at)

    total = send[col]
    if later:
        for copy in copies[2:] + later:
            copy.wait_recv()
        total = total + arrive[1] + arrive[2]
    else:
        for copy in copies:
            copy.wait_recv()
        for step in range(n_col - 1):
            total = total + arrive[step]
    solved = exact_dot(total, matrix)
    for i in range(edge):
        out_ref[:, i : i + 1, :] = solved[i * IB_DEV : (i + 1) * IB_DEV][:, None, :]

    for copy in copies + later:
        copy.wait_send()
    for step in range(1, n_row):
        normal_copy(step, row).wait_send()
    for step in range(1, n_col):
        gram_copy(step, 0).wait_send()
        gram_copy(step, 1).wait_send()
    pair_copy(0, row).wait_send()
    for step in range(chips - 1):
        for way in range(2):

            @pl.when(has(way, step))
            def _():
                pair_copy(1 + 2 * step + way, sent_chip(way, step + 1) * 2 + core).wait_send()

            @pl.when(sends(way, step))
            def _():
                line_copy(way, step, sent_chip(way, step), next_chip(way)).wait_send()


def local(
    n_row,
    n_col,
    tile_values,
    tile_count,
    mode1_column,
    mode1_offset,
    mode2_row,
    mode2_offset,
    mode3_offset,
    mode2_factor,
    mode3_factor,
):
    slots, edge = tile_values.shape[0], tile_values.shape[1]
    rows_held, rank = mode2_factor.shape
    blocks_held = rows_held // edge
    is_live = jnp.arange(slots, dtype=jnp.int32) < tile_count[0]
    index = jnp.stack([mode2_row[:, 0] * blocks_held + mode2_offset, mode3_offset])
    target = jnp.where(is_live, mode1_column[:, 0] * IB_DEV + mode1_offset, -1)[None, :]
    live = is_live.astype(jnp.int32)[:, None]
    rows_out = IB_DEV * edge
    piece = rank // n_row
    chips = n_row // 2
    f32, bf16 = jnp.float32, jnp.bfloat16
    dma = pltpu.SemaphoreType.DMA
    vmem = pl.BlockSpec(memory_space=pltpu.VMEM)
    smem = pl.BlockSpec(memory_space=pltpu.SMEM)
    blocks = max(6, n_col - 1)
    out = pl.pallas_call(
        functools.partial(kernel, n_row, n_col),
        out_shape=jax.ShapeDtypeStruct((IB_DEV, edge, rank), f32),
        in_specs=[smem, vmem, vmem, pl.BlockSpec(memory_space=pl.ANY), vmem, vmem],
        out_specs=vmem,
        scratch_shapes=[
            pltpu.VMEM(tile_values.shape, f32),
            pltpu.VMEM((n_row * blocks_held, edge, rank), f32),
            pltpu.VMEM((mode3_factor.shape[0] // edge, edge, rank), bf16),
            pltpu.VMEM((mode3_factor.shape[0] // edge, edge, rank), bf16),
            pltpu.VMEM((rank, rank), f32),
            pltpu.VMEM((rank, rank), f32),
            pltpu.VMEM((2, n_col, piece, rank), f32),
            pltpu.VMEM((n_row, piece, rank), f32),
            pltpu.VMEM((edge, slots, rank), f32),
            pltpu.VMEM((n_col, rows_out, rank), f32),
            pltpu.VMEM((max(3, n_col - 1), rows_out, rank), f32),
            dma,
            dma((2, chips)),
            dma((2, chips)),
            dma((2 * chips,)),
            dma((2 * chips,)),
            dma((2, n_col)),
            dma((2, n_col)),
            dma((n_row,)),
            dma((n_row,)),
            dma((blocks,)),
            dma((blocks,)),
        ],
        compiler_params=pltpu.CompilerParams(
            collective_id=0, has_side_effects=True, vmem_limit_bytes=52 * 2**20
        ),
    )(index, live, target, tile_values, mode2_factor, mode3_factor)
    return out.reshape(rows_out, rank)


def solution(mesh):
    placed = (
        P(("row", "col"), None, None),
        P(("row", "col")),
        P(("row", "col"), None),
        P(("row", "col")),
        P(("row", "col"), None),
        P(("row", "col")),
        P(("row", "col")),
        P(("row", "col"), None),
        P("col", None),
    )
    return jax.shard_map(
        functools.partial(local, mesh.shape["row"], mesh.shape["col"]),
        mesh=mesh,
        in_specs=placed,
        out_specs=P(("row", "col"), None),
        check_vma=False,
    )
```

time: 285 us -> 95.9 us (0.34)
  waiting for transfers between devices: 125 us -> 0 us
  Pallas kernels: 0 us -> 90.2 us
  other arithmetic: 64.2 us -> 2.02 us
  matrix products: 42.6 us -> 0 us
  local copies, waits for them, and re-layouts: 24.2 us -> 2.78 us
  between operations: 18 us -> 0.67 us
  blocking collectives: 9.98 us -> 0 us
    pallas_call x0 -> x1, Pallas kernels: none -> 90.2 us  [local(): pl.pallas_call(functools.partial(kernel, n_row, n_col), out_shape=jax.Sha...]
    psum x2 -> x0, waiting for transfers between devices: 89.5 us -> none  [the longest x1 45.2 us: local(): sum_second = lax.psum(own_second, ('row', 'col'))]
    another operation x9 -> x2, other arithmetic: 53.9 us -> 1.34 us  [local(): jnp.stack([mode2_row[:, 0] * blocks_held + mode2_offset, mode3_offset])]
    dot_general x8 -> x0, matrix products: 39.6 us -> none  [the longest x5 30.5 us: contract(): jnp.einsum('gie,ger->gir', values_part, khatri, precision=HIGHEST_PRECISION)]
    all_gather x2 -> x0, waiting for transfers between devices: 34.5 us -> none  [the longest x1 23.7 us: local(): shard_piece = lax.all_gather(mode2_factor, 'row', axis=0, tiled=True)]
    unnamed x1 -> x0, blocking collectives: 9.98 us -> none
    gather x2 -> x0, local copies, waits for them, and re-layouts: 8.92 us -> none  [the longest x1 5.25 us: local(): jnp.take(shard_piece, jnp.clip(wanted, 0, piece_length - 1).reshape(-1),...]
    mul x7 -> x0, other arithmetic: 6.83 us -> none  [the longest x5 5.76 us: contract(): second_part[:, :, None, :] * third_part[:, None, :, :]]
  transfers between devices with their start and end apart: 4 -> 0, of which waited for: 4 -> 0; matrix products, arithmetic and copies ran while one was open for 43% -> 0% of each run, Pallas kernels for 0% -> 0%
where the time goes in v1:
time: 95.9 us; the launch traced here: 95.7 us
  Pallas kernels  90.2 us (94%)
  local copies, waits for them, and re-layouts  2.78 us (3%)
  other arithmetic  2.02 us (2%)
    pallas_call x1, Pallas kernels, local(): pl.pallas_call(functools.partial(kernel, n_row, n_col), out_shape=jax.Sha...  90.2 us
    unnamed x5, local copies, waits for them, and re-layouts  2.78 us

profile of v1, /device:TPU:0, one launch (start us, length us, event | category | flops | bytes accessed | tf_op | source)
XLA Modules:
  0.0 95.7 jit_solution(9331491151051071779)
XLA Ops:
  0.7 0.7 fusion.1.target_ref
  1.3 0.7 fusion.2
  2.0 0.7 pad_add_fusion.index_ref
  2.7 0.0 copy-start
  2.7 1.0 %copy-done = f32[512,256]{1,0:T(8,128)S(1)} copy-done((f32[512,256]{1,0:T(8,128)S(1)}, f32[512,256]{1,0:T(8,128)}, u32[]{:S(2)}) %copy-start) | copy-done | bytes 524312
  3.7 0.0 copy-start.1
  3.7 0.9 copy-done.1
  4.7 90.2 %shard_map.91 = f32[16,32,256]{2,1,0:T(8,128)S(1)} custom-call(s32[2,48]{1,0:T(2,128)S(1)} %pad_add_fusion.index_ref, s32[48,1]{1,0:T(8,128)S(1)} %fusion.live_ref, s32[1,48]{1,0:T(1,128)S(1)} %fusion.1.target_ref, f32[48,32,1024]{2,1,0:T(8,128)} %x_hbm.1, f32[256,256]{1,0:T(8,128)S(1)} %copy-done.1, f32[512,256]{1,0:T(8,128)S(1)} %copy-done), custom_call_target="tpu_custom_call" | custom-call | tf_op jit(solution)/shard_map/pallas_call | solution.py:412
  94.9 0.8 copy.12
  (1 shorter events, 0.0 us)
Async XLA Ops:
  2.7 1.0 %copy-start = (f32[512,256]{1,0:T(8,128)S(1)}, f32[512,256]{1,0:T(8,128)}, u32[]{:S(2)}) copy-start(f32[512,256]{1,0:T(8,128)} %c_ref.1) | copy-start | bytes 1572868
  3.7 0.9 copy-start.1

commit v2 on v1

--- a/solution.py
+++ b/solution.py
@@ -24,15 +24,22 @@
     return high, (values - high.astype(jnp.float32)).astype(jnp.bfloat16)
 
 
+def split_three(values):
+    high = values.astype(jnp.bfloat16)
+    rest = values - high.astype(jnp.float32)
+    middle = rest.astype(jnp.bfloat16)
+    return high, middle, (rest - middle.astype(jnp.float32)).astype(jnp.bfloat16)
+
+
 def invert_small(block):
     size = block.shape[0]
     line = lax.broadcasted_iota(jnp.int32, (size, size), 0)
     lane = lax.broadcasted_iota(jnp.int32, (size, size), 1)
     lane_row = lax.broadcasted_iota(jnp.int32, (1, size), 1)
     for k in range(size):
-        scale = 1.0 / block[k : k + 1, k : k + 1]
+        column = jnp.broadcast_to(block[:, k : k + 1], (size, size))
+        scale = 1.0 / column[k : k + 1, :]
         row = jnp.where(lane_row == k, scale, block[k : k + 1, :] * scale)
-        column = block[:, k : k + 1]
         kept = jnp.where(lane == k, 0.0, block)
         block = jnp.where(line == k, row, kept - column * row)
     return block
@@ -42,16 +49,29 @@
     size = matrix.shape[0]
     start = at * PIVOT
     rows = matrix[start : start + PIVOT, :]
-    columns = matrix[:, start : start + PIVOT]
     lane = lax.broadcasted_iota(jnp.int32, (PIVOT, size), 1)
     line = lax.broadcasted_iota(jnp.int32, (PIVOT, size), 0)
     inside = (lane >= start) & (lane < start + PIVOT)
     pivot = invert_small(rows[:, start : start + PIVOT])
     unit = jnp.where(lane - start == line, 1.0, 0.0)
-    new_rows = exact_dot(pivot, jnp.where(inside, unit, rows))
+    high, middle, low = split_three(jnp.where(inside, unit, rows))
+    p_high, p_middle, p_low = split_three(pivot)
+    new_rows = jnp.dot(
+        jnp.concatenate([p_high, p_high, p_middle, p_high, p_middle, p_low], axis=1),
+        jnp.concatenate([high, middle, high, low, middle, high], axis=0),
+        preferred_element_type=jnp.float32,
+    )
+    c_high, c_middle, c_low = split_three(jnp.where(lane < start, -rows, rows))
+    high, middle, low = split_three(new_rows)
+    change = lax.dot_general(
+        jnp.concatenate([c_high, c_high, c_middle, c_high, c_middle, c_low], axis=0),
+        jnp.concatenate([high, middle, high, low, middle, high], axis=0),
+        (((0,), (0,)), ((), ())),
+        preferred_element_type=jnp.float32,
+    )
     lane_all = lax.broadcasted_iota(jnp.int32, (size, size), 1)
     inside_all = (lane_all >= start) & (lane_all < start + PIVOT)
-    rest = jnp.where(inside_all, 0.0, matrix) - exact_dot(columns, new_rows)
+    rest = jnp.where(inside_all, 0.0, matrix) - change
     pieces = [rest[:start], new_rows, rest[start + PIVOT :]]
     return jnp.concatenate([piece for piece in pieces if piece.shape[0]], axis=0)
 
@@ -59,15 +79,19 @@
 def kernel(
     n_row,
     n_col,
+    row_most,
+    count_ref,
+    lists_ref,
+    x_hbm,
+    b_hbm,
+    c_hbm,
+    out_ref,
+    lists,
     index_ref,
-    live_ref,
-    target_ref,
-    x_hbm,
-    b_ref,
-    c_ref,
-    out_ref,
     x_ref,
     b_all,
+    b_now,
+    c_ref,
     c_high,
     c_low,
     gram2,
@@ -77,7 +101,7 @@
     partials,
     send,
     arrive,
-    x_sem,
+    load_sem,
     line_send,
     line_recv,
     pair_send,
@@ -94,13 +118,20 @@
     chip, core = row // 2, row % 2
     chips = n_row // 2
     other = chip * 2 + 1 - core
-    slots, edge = x_ref.shape[0], x_ref.shape[1]
-    rank = b_ref.shape[1]
+    edge = x_ref.shape[1]
+    slots = lists.shape[0]
+    per_row = row_most
+    rank = c_ref.shape[1]
     piece = rank // n_row
     rows_out = IB_DEV * edge
-    held_blocks = b_ref.shape[0] // edge
-
-    load_x = pltpu.make_async_copy(x_hbm, x_ref, x_sem)
+    held_blocks = b_hbm.shape[0]
+    own_blocks = pl.ds(row * held_blocks, held_blocks)
+
+    load_b = pltpu.make_async_copy(b_hbm, b_all.at[own_blocks], load_sem.at[0])
+    load_c = pltpu.make_async_copy(c_hbm, c_ref, load_sem.at[1])
+    load_x = pltpu.make_async_copy(x_hbm, x_ref, load_sem.at[2])
+    load_b.start()
+    load_c.start()
     load_x.start()
 
     barrier = pltpu.get_barrier_semaphore()
@@ -112,7 +143,30 @@
         pl.semaphore_signal(
             barrier, inc=1, device_id=(row, (col + step) % n_col), device_id_type=MESH
         )
-    b_all[pl.ds(row * held_blocks, held_blocks)] = b_ref[...].reshape(held_blocks, edge, rank)
+    tiles = lists_ref.shape[1]
+    tile_line = lax.broadcasted_iota(jnp.int32, (tiles, tiles), 0)
+    tile_lane = lax.broadcasted_iota(jnp.int32, (tiles, tiles), 1)
+    owner = lists_ref[0:1, :]
+    owner_line = jnp.sum(
+        jnp.where(tile_line == tile_lane, owner, 0), axis=1, keepdims=True, dtype=jnp.int32
+    )
+    before = (owner_line == owner) & (tile_line < tile_lane)
+    place = owner * row_most + jnp.sum(
+        jnp.where(before, 1, 0), axis=0, keepdims=True, dtype=jnp.int32
+    )
+    taken = lax.broadcasted_iota(jnp.int32, (slots, tiles), 0) == place
+    number = lax.broadcasted_iota(jnp.int32, (1, tiles), 1)
+    code = jnp.where(number < count_ref[0], lists_ref[3:4, :] * IB_DEV + lists_ref[4:5, :] + 1, 0)
+    list_lane = lax.broadcasted_iota(jnp.int32, lists.shape, 1)
+    table = jnp.zeros(lists.shape, jnp.int32)
+    for which, values in enumerate((number, lists_ref[1:2, :], lists_ref[2:3, :], code)):
+        listed = jnp.sum(jnp.where(taken, values, 0), axis=1, keepdims=True, dtype=jnp.int32)
+        table = jnp.where(list_lane == which, listed, table)
+    lists[...] = table
+    load_lists = pltpu.make_async_copy(lists, index_ref, load_sem.at[3])
+    load_lists.start()
+
+    load_b.wait()
     pl.semaphore_wait(barrier, n_row + n_col - 2)
 
     def line_copy(way, step, slot_chip, to_chip):
@@ -159,75 +213,28 @@
 
     pair_copy(0, row).start()
 
+    load_c.wait()
     third = c_ref[...]
     high, low = split(third)
     c_high[...] = high.reshape(c_high.shape)
     c_low[...] = low.reshape(c_low.shape)
     gram3[...] = exact_dot(third, third, ((0,), (0,)))
-    own = b_ref[...]
-    gram2[...] = exact_dot(own, own, ((0,), (0,)))
-    pair_copy(0, other).wait_recv()
-
-    def add_gram(slot_row):
-        block = b_all[pl.ds(slot_row * held_blocks, held_blocks)].reshape(b_ref.shape)
-        gram2[...] += exact_dot(block, block, ((0,), (0,)))
-
-    add_gram(other)
-    for step in range(chips - 1):
-        for way in range(2):
-
-            @pl.when(has(way, step))
-            def _():
-                held = sent_chip(way, step + 1)
-                line_copy(way, step, held, next_chip(way)).wait_recv()
-                pair_copy(1 + 2 * step + way, held * 2 + core).start()
-
-            if step + 1 < chips - 1:
-
-                @pl.when(sends(way, step + 1))
-                def _():
-                    line_copy(way, step + 1, sent_chip(way, step + 1), next_chip(way)).start()
-
-        for way in range(2):
-
-            @pl.when(has(way, step))
-            def _():
-                held = sent_chip(way, step + 1)
-                add_gram(held * 2 + core)
-                pair_copy(1 + 2 * step + way, held * 2 + 1 - core).wait_recv()
-                add_gram(held * 2 + 1 - core)
-
-    def gram_copy(step, which):
-        to_col = (col + step) % n_col
-        source = gram2 if which == 0 else gram3
-        return pltpu.make_async_remote_copy(
-            src_ref=source.at[pl.ds(pl.multiple_of(row * piece, 8), piece)],
-            dst_ref=gram_in.at[which, step],
-            send_sem=gram_send.at[which, step],
-            recv_sem=gram_recv.at[which, step],
-            device_id=(row, to_col),
-            device_id_type=MESH,
-        )
-
-    for step in range(1, n_col):
-        gram_copy(step, 0).start()
-        gram_copy(step, 1).start()
-
+    gram2[...] = jnp.zeros_like(gram2)
     load_x.wait()
+    load_lists.wait()
     lane = lax.broadcasted_iota(jnp.int32, (edge, 128), 1)
     lane_row = lax.broadcasted_iota(jnp.int32, (1, 128), 1) // edge
     one_mask = [jnp.where(lane_row == m, 1.0, 0.0).astype(jnp.bfloat16) for m in range(4)]
     two_mask = [jnp.where(lane_row % 2 == m, 1.0, 0.0).astype(jnp.bfloat16) for m in range(2)]
     chunks = edge * edge // 128
 
-    def tile(t, carried):
-        third_at = index_ref[1, t]
-        weights_high = c_high[third_at]
-        weights_low = c_low[third_at]
-        weights = jnp.concatenate([weights_high] * 6 + [weights_low] * 2, axis=0)
+    def tile(slot, second):
+        third_at = index_ref[slot, 2]
+        tile_at = index_ref[slot, 0]
+        weights = jnp.concatenate([c_high[third_at]] * 6 + [c_low[third_at]] * 2, axis=0)
         pieces = []
         for q in range(chunks):
-            x = x_ref[t, :, q * 128 : (q + 1) * 128]
+            x = x_ref[tile_at, :, q * 128 : (q + 1) * 128]
             first = x.astype(jnp.bfloat16)
             x_high = first.astype(jnp.float32)
             x_low = x - x_high
@@ -243,14 +250,75 @@
         inner = jnp.dot(
             jnp.concatenate(pieces, axis=0), weights, preferred_element_type=jnp.float32
         )
-        second = b_all[index_ref[0, t]]
         total = inner[:edge] * second[0:1]
         for j in range(1, edge):
             total = total + inner[j * edge : (j + 1) * edge] * second[j : j + 1]
-        partials[:, pl.ds(t, 1), :] = total[:, None, :]
+        partials[:, pl.ds(slot, 1), :] = total[:, None, :]
+
+    def use(held_chip):
+        for side in range(2):
+            held = b_all[pl.ds((held_chip * 2 + side) * held_blocks, held_blocks)]
+            b_now[side] = held
+            flat = held.reshape(held_blocks * edge, rank)
+            gram2[...] += exact_dot(flat, flat, ((0,), (0,)))
+
+    def tiles_of(held_chip):
+        def pair(s, carried):
+            for side in range(2):
+                slot = (held_chip * 2 + side) * per_row + s
+                tile(slot, b_now[side, index_ref[slot, 1]])
+            return carried
+
+        lax.fori_loop(0, per_row, pair, 0)
+
+    def gram_copy(step, which):
+        to_col = (col + step) % n_col
+        source = gram2 if which == 0 else gram3
+        return pltpu.make_async_remote_copy(
+            src_ref=source.at[pl.ds(pl.multiple_of(row * piece, 8), piece)],
+            dst_ref=gram_in.at[which, step],
+            send_sem=gram_send.at[which, step],
+            recv_sem=gram_recv.at[which, step],
+            device_id=(row, to_col),
+            device_id_type=MESH,
+        )
+
+    nearer = jnp.minimum(chip, chips - 1 - chip)
+
+    def turn(number, carried):
+        step = number - 1
+        for way in range(2):
+
+            @pl.when((number > 0) & has(way, step))
+            def _():
+                held = sent_chip(way, step + 1)
+                line_copy(way, step, held, next_chip(way)).wait_recv()
+
+                @pl.when((step + 1 < chips - 1) & sends(way, step + 1))
+                def _():
+                    line_copy(way, step + 1, held, next_chip(way)).start()
+
+                pair_copy(1 + 2 * step + way, held * 2 + core).start()
+
+        both = jnp.where(number % 2 == 1, chip - (number + 1) // 2, chip + number // 2)
+        one = jnp.where(
+            chip < chips - 1 - chip, chip + number - nearer, chip - number + nearer
+        )
+        held = jnp.where(number <= 2 * nearer, both, one)
+        pair_at = jnp.where(held < chip, 2 * (chip - held) - 1, 2 * (held - chip))
+        pair_copy(pair_at, held * 2 + 1 - core).wait_recv()
+        use(held)
+
+        @pl.when(number == chips - 1)
+        def _():
+            for to_step in range(1, n_col):
+                gram_copy(to_step, 0).start()
+                gram_copy(to_step, 1).start()
+
+        tiles_of(held)
         return carried
 
-    lax.fori_loop(0, slots, tile, 0)
+    lax.fori_loop(0, chips, turn, 0)
 
     for step in range(1, n_col):
         gram_copy(step, 0).wait_recv()
@@ -276,24 +344,31 @@
         normal_copy(step, row).start()
 
     targets = n_col * IB_DEV
-    chosen = lax.broadcasted_iota(jnp.int32, (targets, slots), 0) == target_ref[...]
+    code_line = lists[:, 3:4]
+    same = lax.broadcasted_iota(jnp.int32, (slots, slots), 0) == lax.broadcasted_iota(
+        jnp.int32, (slots, slots), 1
+    )
+    code_lane = jnp.sum(jnp.where(same, code_line, 0), axis=0, keepdims=True, dtype=jnp.int32)
+    chosen = lax.broadcasted_iota(jnp.int32, (targets, slots), 0) + 1 == code_lane
     chosen = jnp.where(chosen, 1.0, 0.0)
     chosen = jnp.concatenate([chosen, chosen], axis=1).astype(jnp.bfloat16)
 
-    live = live_ref[...] > 0
-
-    def choose(i, carried):
-        high, low = split(jnp.where(live, partials[i], 0.0))
-        rows = jnp.dot(
-            chosen, jnp.concatenate([high, low], axis=0), preferred_element_type=jnp.float32
-        )
-        for c in range(n_col):
-            send[c, pl.ds(pl.multiple_of(i * IB_DEV, IB_DEV), IB_DEV), :] = rows[
-                c * IB_DEV : (c + 1) * IB_DEV
-            ]
+    live = code_line > 0
+
+    def choose(group, carried):
+        for part in range(4):
+            i = group * 4 + part
+            high, low = split(jnp.where(live, partials[i], 0.0))
+            rows = jnp.dot(
+                chosen, jnp.concatenate([high, low], axis=0), preferred_element_type=jnp.float32
+            )
+            for c in range(n_col):
+                send[c, pl.ds(pl.multiple_of(i * IB_DEV, IB_DEV), IB_DEV), :] = rows[
+                    c * IB_DEV : (c + 1) * IB_DEV
+                ]
         return carried
 
-    lax.fori_loop(0, edge, choose, 0)
+    lax.fori_loop(0, edge // 4, choose, 0)
 
     def block_copy(number, source, target, to_col):
         return pltpu.make_async_remote_copy(
@@ -337,14 +412,15 @@
         normal_copy(step, (row + n_row - step) % n_row).wait_recv()
     matrix = jnp.concatenate([normal_in[r] for r in range(n_row)], axis=0)
     pivots = rank // PIVOT
-    for at in range(pivots // 2):
+    early = 3 * pivots // 8
+    for at in range(early):
         matrix = eliminate(matrix, at)
     if later:
         for way in range(2):
             copies[way].wait_recv()
             send[sides[1 - way], halves[way]] += arrive[0, halves[way]]
             later[way].start()
-    for at in range(pivots // 2, pivots):
+    for at in range(early, pivots):
         matrix = eliminate(matrix, at)
 
     total = send[col]
@@ -397,10 +473,11 @@
     slots, edge = tile_values.shape[0], tile_values.shape[1]
     rows_held, rank = mode2_factor.shape
     blocks_held = rows_held // edge
-    is_live = jnp.arange(slots, dtype=jnp.int32) < tile_count[0]
-    index = jnp.stack([mode2_row[:, 0] * blocks_held + mode2_offset, mode3_offset])
-    target = jnp.where(is_live, mode1_column[:, 0] * IB_DEV + mode1_offset, -1)[None, :]
-    live = is_live.astype(jnp.int32)[:, None]
+    row_most = {8: 7, 16: 4}.get(n_row, slots)
+    places = n_row * row_most
+    lists = jnp.stack(
+        [mode2_row[:, 0], mode2_offset, mode3_offset, mode1_column[:, 0], mode1_offset]
+    )
     rows_out = IB_DEV * edge
     piece = rank // n_row
     chips = n_row // 2
@@ -408,25 +485,30 @@
     dma = pltpu.SemaphoreType.DMA
     vmem = pl.BlockSpec(memory_space=pltpu.VMEM)
     smem = pl.BlockSpec(memory_space=pltpu.SMEM)
+    hbm = pl.BlockSpec(memory_space=pltpu.HBM)
     blocks = max(6, n_col - 1)
     out = pl.pallas_call(
-        functools.partial(kernel, n_row, n_col),
+        functools.partial(kernel, n_row, n_col, row_most),
         out_shape=jax.ShapeDtypeStruct((IB_DEV, edge, rank), f32),
-        in_specs=[smem, vmem, vmem, pl.BlockSpec(memory_space=pl.ANY), vmem, vmem],
+        in_specs=[smem, vmem, hbm, hbm, hbm],
         out_specs=vmem,
         scratch_shapes=[
+            pltpu.VMEM((places, 128), jnp.int32),
+            pltpu.SMEM((places, 128), jnp.int32),
             pltpu.VMEM(tile_values.shape, f32),
             pltpu.VMEM((n_row * blocks_held, edge, rank), f32),
+            pltpu.VMEM((2, blocks_held, edge, rank), f32),
+            pltpu.VMEM(mode3_factor.shape, f32),
             pltpu.VMEM((mode3_factor.shape[0] // edge, edge, rank), bf16),
             pltpu.VMEM((mode3_factor.shape[0] // edge, edge, rank), bf16),
             pltpu.VMEM((rank, rank), f32),
             pltpu.VMEM((rank, rank), f32),
             pltpu.VMEM((2, n_col, piece, rank), f32),
             pltpu.VMEM((n_row, piece, rank), f32),
-            pltpu.VMEM((edge, slots, rank), f32),
+            pltpu.VMEM((edge, places, rank), f32),
             pltpu.VMEM((n_col, rows_out, rank), f32),
             pltpu.VMEM((max(3, n_col - 1), rows_out, rank), f32),
-            dma,
+            dma((4,)),
             dma((2, chips)),
             dma((2, chips)),
             dma((2 * chips,)),
@@ -439,9 +521,9 @@
             dma((blocks,)),
         ],
         compiler_params=pltpu.CompilerParams(
-            collective_id=0, has_side_effects=True, vmem_limit_bytes=52 * 2**20
+            collective_id=0, has_side_effects=True, vmem_limit_bytes=60 * 2**20
         ),
-    )(index, live, target, tile_values, mode2_factor, mode3_factor)
+    )(tile_count, lists, tile_values, mode2_factor.reshape(blocks_held, edge, rank), mode3_factor)
     return out.reshape(rows_out, rank)
 
 

time: 95.9 us -> 77 us (0.80)
  Pallas kernels: 90.2 us -> 72.9 us
  other arithmetic: 2.02 us -> 0 us
    pallas_call x1, Pallas kernels: 90.2 us -> 72.9 us  [local(): pl.pallas_call(functools.partial(kernel, n_row, n_col, row_most), out_sha...]
    another operation x2 -> x0, other arithmetic: 1.34 us -> none  [local(): jnp.stack([mode2_row[:, 0] * blocks_held + mode2_offset, mode3_offset])]
    another operation x0 -> x1, local copies, waits for them, and re-layouts: none -> 1.32 us  [local(): jnp.stack([mode2_row[:, 0], mode2_offset, mode3_offset, mode1_column[:, 0...]
    unnamed x5 -> x1, local copies, waits for them, and re-layouts: 2.78 us -> 1.87 us
where the time goes in v2:
time: 77 us; the launch traced here: 76.8 us
  Pallas kernels  72.9 us (95%)
  local copies, waits for them, and re-layouts  3.19 us (4%)
    pallas_call x1, Pallas kernels, local(): pl.pallas_call(functools.partial(kernel, n_row, n_col, row_most), out_sha...  72.9 us
    unnamed x1, local copies, waits for them, and re-layouts  1.87 us

profile of v2, /device:TPU:0, one launch (start us, length us, event | category | flops | bytes accessed | tf_op | source)
XLA Modules:
  0.0 76.8 jit_solution(18035021605925619092)
XLA Ops:
  0.7 1.3 %stack.15.lists_ref = s32[5,48]{1,0:T(8,128)} concatenate(s32[1,48]{1,0:T(1,128)} %bitcast.9, s32[1,48]{1,0:T(1,128)} %bitcast.10, s32[1,48]{1,0:T(1,128)} %bitcast.11, s32[1,48]{1,0:T(1,128)} %bitcast.12, s32[1,48]{1,0:T(1,128)} %bitcast.13), dimensions={0} | concatenate | bytes 1920 | tf_op jit(solution)/shard_map/stack | solution.py:478
  2.0 72.9 %shard_map.91 = f32[16,32,256]{2,1,0:T(8,128)} custom-call(s32[1]{0:T(128)S(6)} %copy.11.count_ref, s32[5,48]{1,0:T(8,128)} %stack.15.lists_ref, f32[48,32,1024]{2,1,0:T(8,128)} %x_hbm.1, f32[8,32,256]{2,1,0:T(8,128)} %bitcast.8, f32[512,256]{1,0:T(8,128)} %c_hbm.1), custom_call_target="tpu_custom_call" | custom-call | tf_op jit(solution)/shard_map/pallas_call | solution.py:490
  74.9 1.9 %copy.12 = f32[512,256]{1,0:T(8,128)} copy(f32[512,256]{1,0:T(8,128)} %bitcast.7) | data formatting | bytes 1048576

commit v3 on v2

--- a/solution.py
+++ b/solution.py
@@ -9,6 +9,7 @@
 
 IB_DEV = 16
 PIVOT = 32
+SPREAD = 8
 MESH = pl.DeviceIdType.MESH
 HIGHEST = lax.Precision.HIGHEST
 
@@ -36,19 +37,26 @@
     line = lax.broadcasted_iota(jnp.int32, (size, size), 0)
     lane = lax.broadcasted_iota(jnp.int32, (size, size), 1)
     lane_row = lax.broadcasted_iota(jnp.int32, (1, size), 1)
-    for k in range(size):
-        column = jnp.broadcast_to(block[:, k : k + 1], (size, size))
-        scale = 1.0 / column[k : k + 1, :]
-        row = jnp.where(lane_row == k, scale, block[k : k + 1, :] * scale)
-        kept = jnp.where(lane == k, 0.0, block)
-        block = jnp.where(line == k, row, kept - column * row)
+    for first in range(0, size, SPREAD):
+        columns = [
+            jnp.broadcast_to(block[:, k : k + 1], (size, size))
+            for k in range(first, first + SPREAD)
+        ]
+        for k in range(first, first + SPREAD):
+            column = columns[k - first]
+            scale = 1.0 / column[k : k + 1, :]
+            row = jnp.where(lane_row == k, scale, block[k : k + 1, :] * scale)
+            kept = jnp.where(lane == k, 0.0, block)
+            block = jnp.where(line == k, row, kept - column * row)
+            for later in range(k + 1 - first, SPREAD):
+                entry = columns[later][k : k + 1, :] * scale
+                columns[later] = jnp.where(line == k, entry, columns[later] - column * entry)
     return block
 
 
-def eliminate(matrix, at):
+def eliminate(matrix, rows, at):
     size = matrix.shape[0]
     start = at * PIVOT
-    rows = matrix[start : start + PIVOT, :]
     lane = lax.broadcasted_iota(jnp.int32, (PIVOT, size), 1)
     line = lax.broadcasted_iota(jnp.int32, (PIVOT, size), 0)
     inside = (lane >= start) & (lane < start + PIVOT)
@@ -63,17 +71,38 @@
     )
     c_high, c_middle, c_low = split_three(jnp.where(lane < start, -rows, rows))
     high, middle, low = split_three(new_rows)
-    change = lax.dot_general(
-        jnp.concatenate([c_high, c_high, c_middle, c_high, c_middle, c_low], axis=0),
-        jnp.concatenate([high, middle, high, low, middle, high], axis=0),
-        (((0,), (0,)), ((), ())),
-        preferred_element_type=jnp.float32,
-    )
+    left = jnp.concatenate([c_high, c_high, c_middle, c_high, c_middle, c_low], axis=0)
+    right = jnp.concatenate([high, middle, high, low, middle, high], axis=0)
+
+    def change(part):
+        return lax.dot_general(
+            part, right, (((0,), (0,)), ((), ())), preferred_element_type=jnp.float32
+        )
+
+    after = start + PIVOT
+    next_rows = None
+    if after < size:
+        next_rows = jnp.where(inside, 0.0, matrix[after : after + PIVOT]) - change(
+            left[:, after : after + PIVOT]
+        )
     lane_all = lax.broadcasted_iota(jnp.int32, (size, size), 1)
-    inside_all = (lane_all >= start) & (lane_all < start + PIVOT)
-    rest = jnp.where(inside_all, 0.0, matrix) - change
-    pieces = [rest[:start], new_rows, rest[start + PIVOT :]]
-    return jnp.concatenate([piece for piece in pieces if piece.shape[0]], axis=0)
+    inside_all = (lane_all >= start) & (lane_all < after)
+    rest = jnp.where(inside_all, 0.0, matrix) - change(left)
+    pieces = [rest[:start], new_rows, rest[after:]]
+    matrix = jnp.concatenate([piece for piece in pieces if piece.shape[0]], axis=0)
+    return matrix, next_rows
+
+
+def add_squares(squares, mixed, values):
+    high, middle = split(values)
+    contract = (((0,), (0,)), ((), ()))
+    both = lax.dot_general(
+        high, jnp.concatenate([high, middle], axis=1), contract, preferred_element_type=jnp.float32
+    )
+    rest = lax.dot_general(middle, middle, contract, preferred_element_type=jnp.float32)
+    width = values.shape[1]
+    squares[...] += both[:, :width] + rest
+    mixed[...] += both[:, width:]
 
 
 def kernel(
@@ -96,6 +125,7 @@
     c_low,
     gram2,
     gram3,
+    mixed,
     gram_in,
     normal_in,
     partials,
@@ -218,8 +248,12 @@
     high, low = split(third)
     c_high[...] = high.reshape(c_high.shape)
     c_low[...] = low.reshape(c_low.shape)
-    gram3[...] = exact_dot(third, third, ((0,), (0,)))
+    gram3[...] = jnp.zeros_like(gram3)
+    mixed[...] = jnp.zeros_like(mixed)
+    add_squares(gram3, mixed, third)
+    gram3[...] += mixed[...] + mixed[...].T
     gram2[...] = jnp.zeros_like(gram2)
+    mixed[...] = jnp.zeros_like(mixed)
     load_x.wait()
     load_lists.wait()
     lane = lax.broadcasted_iota(jnp.int32, (edge, 128), 1)
@@ -260,7 +294,7 @@
             held = b_all[pl.ds((held_chip * 2 + side) * held_blocks, held_blocks)]
             b_now[side] = held
             flat = held.reshape(held_blocks * edge, rank)
-            gram2[...] += exact_dot(flat, flat, ((0,), (0,)))
+            add_squares(gram2, mixed, flat)
 
     def tiles_of(held_chip):
         def pair(s, carried):
@@ -311,6 +345,7 @@
 
         @pl.when(number == chips - 1)
         def _():
+            gram2[...] += mixed[...] + mixed[...].T
             for to_step in range(1, n_col):
                 gram_copy(to_step, 0).start()
                 gram_copy(to_step, 1).start()
@@ -412,16 +447,17 @@
         normal_copy(step, (row + n_row - step) % n_row).wait_recv()
     matrix = jnp.concatenate([normal_in[r] for r in range(n_row)], axis=0)
     pivots = rank // PIVOT
+    rows = matrix[:PIVOT]
     early = 3 * pivots // 8
     for at in range(early):
-        matrix = eliminate(matrix, at)
+        matrix, rows = eliminate(matrix, rows, at)
     if later:
         for way in range(2):
             copies[way].wait_recv()
             send[sides[1 - way], halves[way]] += arrive[0, halves[way]]
             later[way].start()
     for at in range(early, pivots):
-        matrix = eliminate(matrix, at)
+        matrix, rows = eliminate(matrix, rows, at)
 
     total = send[col]
     if later:
@@ -503,6 +539,7 @@
             pltpu.VMEM((mode3_factor.shape[0] // edge, edge, rank), bf16),
             pltpu.VMEM((rank, rank), f32),
             pltpu.VMEM((rank, rank), f32),
+            pltpu.VMEM((rank, rank), f32),
             pltpu.VMEM((2, n_col, piece, rank), f32),
             pltpu.VMEM((n_row, piece, rank), f32),
             pltpu.VMEM((edge, places, rank), f32),

time: 77 us -> 62.3 us (0.81)
  Pallas kernels: 72.9 us -> 58.2 us
    pallas_call x1, Pallas kernels: 72.9 us -> 58.2 us  [local(): pl.pallas_call(functools.partial(kernel, n_row, n_col, row_most), out_sha...]
where the time goes in v3:
time: 62.3 us; the launch traced here: 62.1 us
  Pallas kernels  58.2 us (93%)
  local copies, waits for them, and re-layouts  3.19 us (5%)
  between operations  0.66 us (1%)
    pallas_call x1, Pallas kernels, local(): pl.pallas_call(functools.partial(kernel, n_row, n_col, row_most), out_sha...  58.2 us
    unnamed x1, local copies, waits for them, and re-layouts  1.87 us
    another operation x1, local copies, waits for them, and re-layouts, local(): jnp.stack([mode2_row[:, 0], mode2_offset, mode3_offset, mode1_column[:, 0...  1.32 us

profile of v3, /device:TPU:0, one launch (start us, length us, event | category | flops | bytes accessed | tf_op | source)
XLA Modules:
  0.0 62.1 jit_solution(2914600140778351998)
XLA Ops:
  0.7 1.3 %stack.15.lists_ref = s32[5,48]{1,0:T(8,128)} concatenate(s32[1,48]{1,0:T(1,128)} %bitcast.9, s32[1,48]{1,0:T(1,128)} %bitcast.10, s32[1,48]{1,0:T(1,128)} %bitcast.11, s32[1,48]{1,0:T(1,128)} %bitcast.12, s32[1,48]{1,0:T(1,128)} %bitcast.13), dimensions={0} | concatenate | bytes 1920 | tf_op jit(solution)/shard_map/stack | solution.py:514
  2.0 58.2 %shard_map.91 = f32[16,32,256]{2,1,0:T(8,128)} custom-call(s32[1]{0:T(128)S(6)} %copy.11.count_ref, s32[5,48]{1,0:T(8,128)} %stack.15.lists_ref, f32[48,32,1024]{2,1,0:T(8,128)} %x_hbm.1, f32[8,32,256]{2,1,0:T(8,128)} %bitcast.8, f32[512,256]{1,0:T(8,128)} %c_hbm.1), custom_call_target="tpu_custom_call" | custom-call | tf_op jit(solution)/shard_map/pallas_call | solution.py:526
  60.2 1.9 %copy.12 = f32[512,256]{1,0:T(8,128)} copy(f32[512,256]{1,0:T(8,128)} %bitcast.7) | data formatting | bytes 1048576

commit v4 on v3

--- a/solution.py
+++ b/solution.py
@@ -10,6 +10,7 @@
 IB_DEV = 16
 PIVOT = 32
 SPREAD = 8
+PIECES = 4
 MESH = pl.DeviceIdType.MESH
 HIGHEST = lax.Precision.HIGHEST
 
@@ -110,7 +111,11 @@
     n_col,
     row_most,
     count_ref,
-    lists_ref,
+    owner_ref,
+    second_ref,
+    third_ref,
+    target_col_ref,
+    target_ref,
     x_hbm,
     b_hbm,
     c_hbm,
@@ -173,10 +178,10 @@
         pl.semaphore_signal(
             barrier, inc=1, device_id=(row, (col + step) % n_col), device_id_type=MESH
         )
-    tiles = lists_ref.shape[1]
+    tiles = owner_ref.shape[1]
     tile_line = lax.broadcasted_iota(jnp.int32, (tiles, tiles), 0)
     tile_lane = lax.broadcasted_iota(jnp.int32, (tiles, tiles), 1)
-    owner = lists_ref[0:1, :]
+    owner = owner_ref[...]
     owner_line = jnp.sum(
         jnp.where(tile_line == tile_lane, owner, 0), axis=1, keepdims=True, dtype=jnp.int32
     )
@@ -186,10 +191,10 @@
     )
     taken = lax.broadcasted_iota(jnp.int32, (slots, tiles), 0) == place
     number = lax.broadcasted_iota(jnp.int32, (1, tiles), 1)
-    code = jnp.where(number < count_ref[0], lists_ref[3:4, :] * IB_DEV + lists_ref[4:5, :] + 1, 0)
+    code = jnp.where(number < count_ref[0], target_col_ref[...] * IB_DEV + target_ref[...] + 1, 0)
     list_lane = lax.broadcasted_iota(jnp.int32, lists.shape, 1)
     table = jnp.zeros(lists.shape, jnp.int32)
-    for which, values in enumerate((number, lists_ref[1:2, :], lists_ref[2:3, :], code)):
+    for which, values in enumerate((number, second_ref[...], third_ref[...], code)):
         listed = jnp.sum(jnp.where(taken, values, 0), axis=1, keepdims=True, dtype=jnp.int32)
         table = jnp.where(list_lane == which, listed, table)
     lists[...] = table
@@ -390,6 +395,16 @@
 
     live = code_line > 0
 
+    def block_copy(number, source, target, to_col):
+        return pltpu.make_async_remote_copy(
+            src_ref=source,
+            dst_ref=target,
+            send_sem=block_send.at[number],
+            recv_sem=block_recv.at[number],
+            device_id=(row, to_col),
+            device_id_type=MESH,
+        )
+
     def choose(group, carried):
         for part in range(4):
             i = group * 4 + part
@@ -403,44 +418,33 @@
                 ]
         return carried
 
-    lax.fori_loop(0, edge // 4, choose, 0)
-
-    def block_copy(number, source, target, to_col):
-        return pltpu.make_async_remote_copy(
-            src_ref=source,
-            dst_ref=target,
-            send_sem=block_send.at[number],
-            recv_sem=block_recv.at[number],
-            device_id=(row, to_col),
-            device_id_type=MESH,
-        )
-
-    half = rows_out // 2
-    halves = (pl.ds(0, half), pl.ds(half, half))
-    copies = []
-    later = []
+    lines = edge // PIECES
+    length = lines * IB_DEV
+    pieces = [pl.ds(number * length, length) for number in range(PIECES)]
+    corners, beside, later = [], [], []
     if n_col == 4:
         near = (col // 2) * 2 + 1 - col % 2
         far = (1 - col // 2) * 2 + col % 2
         corner = (1 - col // 2) * 2 + 1 - col % 2
         sides = (near, far)
-        for way in range(2):
-            copies.append(
-                block_copy(way, send.at[corner, halves[way]], arrive.at[0, halves[way]], sides[way])
+        for number, held in enumerate(pieces):
+            first, second = sides[number % 2], sides[1 - number % 2]
+            corners.append(block_copy(number, send.at[corner, held], arrive.at[0, held], first))
+            beside.append(
+                block_copy(PIECES + number, send.at[first, held], arrive.at[1, held], first)
             )
-        for way in range(2):
-            copies.append(
-                block_copy(2 + way, send.at[sides[way], halves[way]], arrive.at[1, halves[way]], sides[way])
-            )
-        for way in range(2):
             later.append(
-                block_copy(4 + way, send.at[sides[1 - way], halves[way]], arrive.at[2, halves[way]], sides[1 - way])
+                block_copy(2 * PIECES + number, send.at[second, held], arrive.at[2, held], second)
             )
     else:
         for step in range(1, n_col):
             to_col = (col + step) % n_col
-            copies.append(block_copy(step - 1, send.at[to_col], arrive.at[step - 1], to_col))
-    for copy in copies:
+            beside.append(block_copy(step - 1, send.at[to_col], arrive.at[step - 1], to_col))
+    for number in range(PIECES):
+        lax.fori_loop(number * lines // 4, (number + 1) * lines // 4, choose, 0)
+        if corners:
+            corners[number].start()
+    for copy in beside:
         copy.start()
 
     for step in range(1, n_row):
@@ -448,32 +452,34 @@
     matrix = jnp.concatenate([normal_in[r] for r in range(n_row)], axis=0)
     pivots = rank // PIVOT
     rows = matrix[:PIVOT]
-    early = 3 * pivots // 8
-    for at in range(early):
+    for at in range(pivots):
         matrix, rows = eliminate(matrix, rows, at)
-    if later:
-        for way in range(2):
-            copies[way].wait_recv()
-            send[sides[1 - way], halves[way]] += arrive[0, halves[way]]
-            later[way].start()
-    for at in range(early, pivots):
-        matrix, rows = eliminate(matrix, rows, at)
-
-    total = send[col]
-    if later:
-        for copy in copies[2:] + later:
+        for number in range(len(later)):
+            if at == (1 + 2 * (number // 2)) * pivots // 8:
+                held, second = pieces[number], sides[1 - number % 2]
+                corners[number].wait_recv()
+                send[second, held] += arrive[0, held]
+                later[number].start()
+
+    if not later:
+        for copy in beside:
             copy.wait_recv()
-        total = total + arrive[1] + arrive[2]
-    else:
-        for copy in copies:
-            copy.wait_recv()
-        for step in range(n_col - 1):
-            total = total + arrive[step]
-    solved = exact_dot(total, matrix)
-    for i in range(edge):
-        out_ref[:, i : i + 1, :] = solved[i * IB_DEV : (i + 1) * IB_DEV][:, None, :]
-
-    for copy in copies + later:
+    for number, held in enumerate(pieces):
+        total = send[col, held]
+        if later:
+            beside[number].wait_recv()
+            later[number].wait_recv()
+            total = total + arrive[1, held] + arrive[2, held]
+        else:
+            for step in range(n_col - 1):
+                total = total + arrive[step, held]
+        solved = exact_dot(total, matrix)
+        for i in range(lines):
+            out_ref[:, pl.ds(number * lines + i, 1), :] = solved[
+                i * IB_DEV : (i + 1) * IB_DEV
+            ][:, None, :]
+
+    for copy in corners + beside + later:
         copy.wait_send()
     for step in range(1, n_row):
         normal_copy(step, row).wait_send()
@@ -511,9 +517,10 @@
     blocks_held = rows_held // edge
     row_most = {8: 7, 16: 4}.get(n_row, slots)
     places = n_row * row_most
-    lists = jnp.stack(
-        [mode2_row[:, 0], mode2_offset, mode3_offset, mode1_column[:, 0], mode1_offset]
-    )
+    lists = [
+        values.reshape(1, slots)
+        for values in (mode2_row, mode2_offset, mode3_offset, mode1_column, mode1_offset)
+    ]
     rows_out = IB_DEV * edge
     piece = rank // n_row
     chips = n_row // 2
@@ -522,11 +529,11 @@
     vmem = pl.BlockSpec(memory_space=pltpu.VMEM)
     smem = pl.BlockSpec(memory_space=pltpu.SMEM)
     hbm = pl.BlockSpec(memory_space=pltpu.HBM)
-    blocks = max(6, n_col - 1)
+    blocks = max(3 * PIECES, n_col - 1)
     out = pl.pallas_call(
         functools.partial(kernel, n_row, n_col, row_most),
         out_shape=jax.ShapeDtypeStruct((IB_DEV, edge, rank), f32),
-        in_specs=[smem, vmem, hbm, hbm, hbm],
+        in_specs=[smem] + [vmem] * 5 + [hbm, hbm, hbm],
         out_specs=vmem,
         scratch_shapes=[
             pltpu.VMEM((places, 128), jnp.int32),
@@ -560,7 +567,7 @@
         compiler_params=pltpu.CompilerParams(
             collective_id=0, has_side_effects=True, vmem_limit_bytes=60 * 2**20
         ),
-    )(tile_count, lists, tile_values, mode2_factor.reshape(blocks_held, edge, rank), mode3_factor)
+    )(tile_count, *lists, tile_values, mode2_factor.reshape(blocks_held, edge, rank), mode3_factor)
     return out.reshape(rows_out, rank)
 
 

time: 62.3 us -> 59 us (0.947)
  Pallas kernels: 58.2 us -> 56.3 us
  local copies, waits for them, and re-layouts: 3.19 us -> 1.87 us
    pallas_call x1, Pallas kernels: 58.2 us -> 56.3 us  [local(): pl.pallas_call(functools.partial(kernel, n_row, n_col, row_most), out_sha...]
    another operation x1 -> x0, local copies, waits for them, and re-layouts: 1.32 us -> none  [local(): jnp.stack([mode2_row[:, 0], mode2_offset, mode3_offset, mode1_column[:, 0...]
where the time goes in v4:
time: 59 us; the launch traced here: 58.8 us
  Pallas kernels  56.3 us (95%)
  local copies, waits for them, and re-layouts  1.87 us (3%)
  between operations  0.66 us (1%)
    pallas_call x1, Pallas kernels, local(): pl.pallas_call(functools.partial(kernel, n_row, n_col, row_most), out_sha...  56.3 us
    unnamed x1, local copies, waits for them, and re-layouts  1.87 us

profile of v4, /device:TPU:0, one launch (start us, length us, event | category | flops | bytes accessed | tf_op | source)
XLA Modules:
  0.0 58.8 jit_solution(14151896139302613159)
XLA Ops:
  0.7 56.3 %shard_map.91 = f32[16,32,256]{2,1,0:T(8,128)} custom-call(s32[1]{0:T(128)S(6)} %copy.11.count_ref, s32[1,48]{1,0:T(1,128)} %bitcast.9, s32[1,48]{1,0:T(1,128)} %bitcast.10, s32[1,48]{1,0:T(1,128)} %bitcast.11, s32[1,48]{1,0:T(1,128)} %bitcast.12, s32[1,48]{1,0:T(1,128)} %bitcast.13, f32[48,32,1024]{2,1,0:T(8,128)} %x_hbm.1, f32[8,32,256]{2,1,0:T(8,128)} %bitcast.8, ...), custom_call_target="tpu_custom_call" | custom-call | tf_op jit(solution)/shard_map/pallas_call | solution.py:533
  57.0 1.9 %copy.12 = f32[512,256]{1,0:T(8,128)} copy(f32[512,256]{1,0:T(8,128)} %bitcast.7) | data formatting | bytes 1048576

commit v5 on v4

--- a/solution.py
+++ b/solution.py
@@ -271,27 +271,30 @@
         third_at = index_ref[slot, 2]
         tile_at = index_ref[slot, 0]
         weights = jnp.concatenate([c_high[third_at]] * 6 + [c_low[third_at]] * 2, axis=0)
-        pieces = []
-        for q in range(chunks):
-            x = x_ref[tile_at, :, q * 128 : (q + 1) * 128]
-            first = x.astype(jnp.bfloat16)
-            x_high = first.astype(jnp.float32)
-            x_low = x - x_high
-            turned_high = pltpu.roll(x_high, 64, 1)
-            turned_low = pltpu.roll(x_low, 64, 1)
-            front = jnp.where(lane < 64, x_low, turned_high).astype(jnp.bfloat16)
-            back = jnp.where(lane < 64, turned_low, x_high).astype(jnp.bfloat16)
-            for m in range(4):
-                rest = front if m < 2 else back
-                pieces.append(
-                    jnp.concatenate([first * one_mask[m], rest * two_mask[m % 2]], axis=1)
-                )
-        inner = jnp.dot(
-            jnp.concatenate(pieces, axis=0), weights, preferred_element_type=jnp.float32
-        )
-        total = inner[:edge] * second[0:1]
-        for j in range(1, edge):
-            total = total + inner[j * edge : (j + 1) * edge] * second[j : j + 1]
+        total = None
+        for part in range(2):
+            pieces = []
+            for q in range(part * chunks // 2, (part + 1) * chunks // 2):
+                x = x_ref[tile_at, :, q * 128 : (q + 1) * 128]
+                first = x.astype(jnp.bfloat16)
+                x_high = first.astype(jnp.float32)
+                x_low = x - x_high
+                turned_high = pltpu.roll(x_high, 64, 1)
+                turned_low = pltpu.roll(x_low, 64, 1)
+                front = jnp.where(lane < 64, x_low, turned_high).astype(jnp.bfloat16)
+                back = jnp.where(lane < 64, turned_low, x_high).astype(jnp.bfloat16)
+                for m in range(4):
+                    rest = front if m < 2 else back
+                    pieces.append(
+                        jnp.concatenate([first * one_mask[m], rest * two_mask[m % 2]], axis=1)
+                    )
+            inner = jnp.dot(
+                jnp.concatenate(pieces, axis=0), weights, preferred_element_type=jnp.float32
+            )
+            for at in range(edge // 2):
+                j = part * edge // 2 + at
+                term = inner[at * edge : (at + 1) * edge] * second[j : j + 1]
+                total = term if total is None else total + term
         partials[:, pl.ds(slot, 1), :] = total[:, None, :]
 
     def use(held_chip):

time: 59 us -> 59.3 us (level)
  no operation moved by 1% of the time
where the time goes in v5:
time: 59.3 us; the launch traced here: 59.1 us
  Pallas kernels  56.6 us (95%)
  local copies, waits for them, and re-layouts  1.87 us (3%)
  between operations  0.66 us (1%)
    pallas_call x1, Pallas kernels, local(): pl.pallas_call(functools.partial(kernel, n_row, n_col, row_most), out_sha...  56.6 us
    unnamed x1, local copies, waits for them, and re-layouts  1.87 us

profile of v5, /device:TPU:0, one launch (start us, length us, event | category | flops | bytes accessed | tf_op | source)
XLA Modules:
  0.0 59.1 jit_solution(10172579325540921435)
XLA Ops:
  0.7 56.6 %shard_map.91 = f32[16,32,256]{2,1,0:T(8,128)} custom-call(s32[1]{0:T(128)S(6)} %copy.11.count_ref, s32[1,48]{1,0:T(1,128)} %bitcast.9, s32[1,48]{1,0:T(1,128)} %bitcast.10, s32[1,48]{1,0:T(1,128)} %bitcast.11, s32[1,48]{1,0:T(1,128)} %bitcast.12, s32[1,48]{1,0:T(1,128)} %bitcast.13, f32[48,32,1024]{2,1,0:T(8,128)} %x_hbm.1, f32[8,32,256]{2,1,0:T(8,128)} %bitcast.8, ...), custom_call_target="tpu_custom_call" | custom-call | tf_op jit(solution)/shard_map/pallas_call | solution.py:536
  57.3 1.9 %copy.12 = f32[512,256]{1,0:T(8,128)} copy(f32[512,256]{1,0:T(8,128)} %bitcast.7) | data formatting | bytes 1048576
